TPU v7x, 128 devices: a whole 4x4x4 slice. The times are simulated.
128 devices in a mesh: slab: 8 (over y, core), grp: 16 (over z, x).
Axes of the slice: x: 4, y: 4, z: 4, core: 2. Of those that a mesh axis runs over, the one named last changes fastest.
Arguments:
- source: bfloat16 [1024, 64, 4096], P(('slab', 'grp')), may hold values from -6 to 6
- momentum: bfloat16 [1024, 64, 4096], P(('slab', 'grp')), may hold values from -6 to 6
- velocity: float32 [1, 3, 64, 128, 64], P(None, None, 'slab', 'grp'), may hold values from -12 to 12
- up_taps: float32 [16], replicated, may hold values from 0.2 to 0.8
- smooth_taps: float32 [17], replicated, may hold values from 0.02 to 0.1
- weights: bfloat16 [2048, 64, 192], P(('slab', 'grp')), may hold values from -0.3 to 1.3
- slot_brick: int32 [128, 16], P('slab'), may hold values from -1 to 127, as said below
Outputs:
- image_out: bfloat16 [2048, 64, 4096], P(('slab', 'grp'))
- momentum_out: bfloat16 [2048, 64, 4096], P(('slab', 'grp'))
Inputs may be any that keep to these rules, and one draw needn't show every extreme that they name: `slot_brick`: row r lists, in rising order of owner, the bricks of its slab (numbered within the slab, brick k held by the slab's device k // 8 along grp) that device r reads, then -1. No device reads two bricks of one owner, no brick is read twice, and in every slab some device fills all 16 slots.
All inputs are finite; a program needn't handle non-finite values.
Results may differ from a plain program's by a relative error of at most 0.006.
Values may be sent and summed in bfloat16 or wider, within the bound.
A program may use at most 192 MiB of HBM per device.

v0:
```python
import jax
import jax.numpy as jnp
from jax import lax
from jax.sharding import PartitionSpec as P

step_time = 0.5
highest = lax.Precision.HIGHEST


def with_halo(x, sides, width):
    for axis, dim in sides:
        peers, length = (lax.axis_size(axis), x.shape[dim])
        up = [(i, (i + 1) % peers) for i in range(peers - 1)]
        down = [(j, i) for i, j in up]
        last = lax.slice_in_dim(x, length - width, length, axis=dim)
        initial = lax.slice_in_dim(x, 0, width, axis=dim)
        before = lax.ppermute(last, axis, up)
        after = lax.ppermute(initial, axis, down)
        x = jnp.concatenate([before, x, after], axis=dim)
    return x


def shape_matrix(up_taps, smooth_taps, brick_edge, window_len):
    row_ids = jnp.arange(brick_edge, dtype=jnp.int32)[:, None, None]
    col_ids = jnp.arange(window_len, dtype=jnp.int32)[None, :, None]
    tap_ids = jnp.arange(17, dtype=jnp.int32)[None, None, :]
    tap_index = row_ids + tap_ids - 8 * col_ids + 12
    inside = (tap_index >= 0) & (tap_index < 16)
    picked = up_taps[jnp.clip(tap_index, 0, 15)]
    weighted = jnp.where(inside, picked * smooth_taps[tap_ids], jnp.zeros_like(picked))
    return jnp.sum(weighted, axis=2)


def difference_matrix(brick_edge):
    row_ids = jnp.arange(brick_edge, dtype=jnp.int32)[:, None]
    col_ids = jnp.arange(brick_edge, dtype=jnp.int32)[None, :]
    lower_id = jnp.maximum(row_ids - 1, 0)
    upper_id = jnp.minimum(row_ids + 1, brick_edge - 1)
    spacing = (upper_id - lower_id).astype(jnp.float32)
    return (
        (col_ids == upper_id).astype(jnp.float32) - (col_ids == lower_id).astype(jnp.float32)
    ) / spacing


def paired_right(matrix):
    return jnp.kron(jnp.eye(2, dtype=matrix.dtype), matrix.T)


def along_depth(matrix, field):
    return jnp.einsum("ai,ijk->ajk", matrix, field, preferred_element_type=jnp.float32)


def along_rows(matrix, field):
    return jnp.einsum("bj,ijk->ibk", matrix, field, preferred_element_type=jnp.float32)


def along_cells(paired, field):
    return jnp.einsum("ijk,kc->ijc", field, paired, preferred_element_type=jnp.float32)


def pull(pair_field, matrices):
    first_pass = along_cells(paired_right(matrices[2]), pair_field).astype(jnp.bfloat16)
    second_pass = along_rows(matrices[1], first_pass).astype(jnp.bfloat16)
    return along_depth(matrices[0], second_pass)


def derivatives(field, difference, paired_diff):
    return (
        along_depth(difference, field),
        along_rows(difference, field),
        along_cells(paired_diff, field),
    )


def advance(pair_field, matrices, velocity_fine, difference, paired_diff):
    brick_edge = pair_field.shape[0]
    pulled = pull(pair_field, matrices)
    rounded = pulled.astype(jnp.bfloat16)
    grads = derivatives(rounded, difference, paired_diff)
    drift_term = (
        velocity_fine[0] * grads[0] + velocity_fine[1] * grads[1] + velocity_fine[2] * grads[2]
    )
    spread = along_depth(difference, (velocity_fine[0] * pulled).astype(jnp.bfloat16))
    spread = spread + along_rows(difference, (velocity_fine[1] * pulled).astype(jnp.bfloat16))
    spread = spread + along_cells(paired_diff, (velocity_fine[2] * pulled).astype(jnp.bfloat16))
    image_half = jnp.arange(2 * brick_edge, dtype=jnp.int32) < brick_edge
    update = jnp.where(image_half, drift_term, spread)
    return (pulled - step_time * update).astype(jnp.bfloat16)


def fine_velocity(window, matrix):
    doubled = jnp.concatenate((matrix, matrix), axis=0)
    first_pass = jnp.einsum("nijk,ck->nijc", window, doubled, precision=highest)
    second_pass = jnp.einsum("nijc,bj->nibc", first_pass, matrix, precision=highest)
    return jnp.einsum("nibc,ai->nabc", second_pass, matrix, precision=highest)


def slot_outputs(pair_field, flat_mats, windows, present, matrix, difference, paired_diff):
    brick_edge = pair_field.shape[0]
    section_count = windows.shape[0]
    matrices = flat_mats.reshape(brick_edge, section_count, 3, brick_edge)
    velocity_fine = fine_velocity(windows[0], matrix)
    section_mats = (matrices[:, 0, 0], matrices[:, 0, 1], matrices[:, 0, 2])
    pair_field = advance(pair_field, section_mats, velocity_fine, difference, paired_diff)
    return jnp.where(present, pair_field, jnp.zeros_like(pair_field))


def send_rows(blocks, picked, present):
    chosen = jnp.take(blocks, picked, axis=0)
    mask_shape = (present.shape[0],) + (1,) * (blocks.ndim - 1)
    return jnp.where(present.reshape(mask_shape), chosen, jnp.zeros_like(chosen))


def local(source, momentum, velocity, up_taps, smooth_taps, weights, slot_brick):
    brick_edge = source.shape[1]
    owned_count = source.shape[0]
    section_count = velocity.shape[0]
    my_index = lax.axis_index("grp")
    coarse_len = brick_edge // 8
    window_len = coarse_len + 4
    matrix = shape_matrix(up_taps, smooth_taps, brick_edge, window_len)
    difference = difference_matrix(brick_edge).astype(jnp.bfloat16)
    paired_diff = paired_right(difference)
    slot_ids = jnp.take(slot_brick, my_index, axis=0)
    slot_live = slot_ids >= 0
    safe_ids = jnp.maximum(slot_ids, 0)
    owner_ids = safe_ids // owned_count
    columns = safe_ids % owned_count
    turn_ids = jnp.arange(owned_count, dtype=jnp.int32)
    own_bricks = my_index * owned_count + turn_ids
    hit_rows = jnp.any(slot_brick[:, :, None] == own_bricks[None, None, :], axis=1)
    picked = jnp.sum(jnp.where(hit_rows, turn_ids[None, :], 0), axis=1)
    present = jnp.any(hit_rows, axis=1)
    cube_shape = (owned_count, brick_edge, brick_edge, brick_edge)
    bricks = jnp.concatenate((source.reshape(cube_shape), momentum.reshape(cube_shape)), axis=3)
    anchor = jnp.zeros((), jnp.int32)
    window_shape = (section_count, 3, window_len, window_len, window_len)
    outgoing = send_rows(bricks, picked, present)
    arrived = lax.all_to_all(outgoing, "grp", split_axis=0, concat_axis=0, tiled=True)
    mine_rows = jnp.take(arrived, owner_ids, axis=0)
    layered = with_halo(velocity, (("slab", 2),), 2)
    coarse_plane = lax.all_gather(layered, "grp", axis=3, tiled=True)
    coarse_plane = jnp.pad(coarse_plane, ((0, 0), (0, 0), (0, 0), (2, 2), (2, 2)))

    def per_slot(inputs):
        pair_field, flat_mats, owner_id, column, live = inputs
        starts = (anchor, anchor, anchor, owner_id * coarse_len, column * coarse_len)
        windows = lax.dynamic_slice(coarse_plane, starts, window_shape)
        return slot_outputs(pair_field, flat_mats, windows, live, matrix, difference, paired_diff)

    results = lax.map(per_slot, (mine_rows, weights, owner_ids, columns, slot_live))
    slot_count = results.shape[0]
    image_out = results[:, :, :, :brick_edge].reshape(
        slot_count, brick_edge, brick_edge * brick_edge
    )
    momentum_out = results[:, :, :, brick_edge:].reshape(
        slot_count, brick_edge, brick_edge * brick_edge
    )
    return (image_out, momentum_out)


def solution(mesh):
    placed = (
        P(("slab", "grp"), None, None),
        P(("slab", "grp"), None, None),
        P(None, None, "slab", "grp", None),
        P(),
        P(),
        P(("slab", "grp"), None, None),
        P("slab", None),
    )
    return jax.shard_map(
        local,
        mesh=mesh,
        in_specs=placed,
        out_specs=(P(("slab", "grp"), None, None), P(("slab", "grp"), None, None)),
        check_vma=False,
    )
```

profile of v0, /device:TPU:16, one launch (start us, length us, event | category | flops | bytes accessed | tf_op | source)
XLA Modules:
  0.0 1052.1 jit_solution(8317389898609324254)
XLA Ops:
  8.8 12.6 %reshape.267 = bf16[8,64,64,64]{3,2,1,0:T(8,128)(2,1)} reshape(bf16[8,64,4096]{2,1,0:T(8,128)(2,1)} %param.9) | data formatting | bytes 8388608 | tf_op jit(solution)/shard_map/reshape | solution.py:135
  21.3 12.5 %reshape.268 = bf16[8,64,64,64]{3,2,1,0:T(8,128)(2,1)} reshape(bf16[8,64,4096]{2,1,0:T(8,128)(2,1)} %param.10) | data formatting | bytes 8388608 | tf_op jit(solution)/shard_map/reshape | solution.py:135
  33.9 10.9 %pad_maximum_fusion = bf16[8,64,64,128]{3,2,1,0:T(8,128)(2,1)} fusion(bf16[8,64,64,64]{3,2,1,0:T(8,128)(2,1)} %reshape.268, bf16[8,64,64,64]{3,2,1,0:T(8,128)(2,1)} %reshape.267), kind=kLoop, calls=%fused_computation.75 | loop fusion | flops 16777216 | bytes 16777216 | tf_op jit(solution)/shard_map/concatenate | solution.py:135
  44.8 10.5 %gather_fusion = bf16[16,64,64,128]{3,2,1,0:T(8,128)(2,1)} fusion(bf16[8,64,64,128]{3,2,1,0:T(8,128)(2,1)} %pad_maximum_fusion, s32[1024]{0:T(1024)S(1)} %pad_clamp_fusion.3), kind=kCustom, calls=%fused_computation | custom fusion | bytes 33554496 | tf_op jit(solution)/shard_map/jit(_take)/gather | solution.py:109
  55.3 14.3 %select_select_fusion = bf16[16,64,64,128]{3,2,1,0:T(8,128)(2,1)} fusion(bf16[16,64,64,128]{3,2,1,0:T(8,128)(2,1)} %gather_fusion, pred[16]{0:T(512)(128)(4,1)S(1)} %compare_and_fusion, pred[16]{0:T(512)(128)(4,1)S(1)} %get-tuple-element.263), kind=kLoop, calls=%fused_computation.73 | loop fusion | flops 16777216 | bytes 33554464 | tf_op jit(solution)/shard_map/jit(_where)/select_n | solution.py:111
  69.6 8.0 all-to-all-start
  85.9 72.7 %gather_fusion.2 = f32[13056]{0:T(1024)S(1)} fusion(f32[16]{0:T(128)S(1)} %copy-done, s32[13312]{0:T(1024)S(1)} %pad_clamp_fusion), kind=kCustom, calls=%fused_computation.2 | custom fusion | bytes 156672 | tf_op jit(solution)/shard_map/gather | solution.py:29
  161.6 175.3 %all-gather.2.cloned.1.call-done = f32[1,3,12,128,64]{4,3,2,1,0:T(8,128)} async-done(((f32[1,3,12,8,64]{4,3,2,1,0:T(8,128)}), f32[1,3,12,128,64]{4,3,2,1,0:T(8,128)}) %all-gather.2.cloned.1.call-update) | async-done | bytes 1179664 | tf_op jit(solution)/shard_map/all_gather | solution.py:142
  340.8 12.9 %gather_fusion.1 = bf16[16,64,64,128]{3,2,1,0:T(8,128)(2,1)} fusion(bf16[16,64,64,128]{3,2,1,0:T(8,128)(2,1)} %all-to-all-done, s32[1024]{0:T(1024)S(1)} %pad_clamp_fusion.2), kind=kCustom, calls=%fused_computation.1 | custom fusion | bytes 33554496 | tf_op jit(solution)/shard_map/jit(_take)/gather | solution.py:140
  353.7 14.1 %broadcast_select_fusion = bf16[16,64,64,128]{3,2,1,0:T(8,128)(2,1)} fusion(bf16[16,64,64,128]{3,2,1,0:T(8,128)(2,1)} %gather_fusion.1, pred[16]{0:T(512)(128)(4,1)S(1)} %get-tuple-element.297), kind=kLoop, calls=%fused_computation.74 | loop fusion | flops 8388608 | bytes 33554448 | tf_op jit(solution)/shard_map/jit(_take)/select_n | solution.py:140
  367.9 581.6 %while.14 = (s32[]{:T(128)}, bf16[16,64,64,128]{3,1,2,0:T(8,128)(2,1)}, pred[16]{0:T(512)(128)(4,1)S(1)}, bf16[16,64,192]{2,1,0:T(8,128)(2,1)}, bf16[16,64,64,12...) while((s32[]{:T(128)}, ...), condition=%wide.region_5.6_spmd.clone.clone, body=%wide.region_4.5_spmd.clone.clone.sunk | while | flops 1093386368 | bytes 66488560 | solution.py:151
  373.0 8.2 convolution_bitcast_fusion.5
  395.1 9.1 fusion.122
  409.3 8.2 convolution_bitcast_fusion.5
  431.4 9.1 fusion.122
  445.6 8.2 convolution_bitcast_fusion.5
  467.8 9.1 fusion.122
  482.0 8.2 convolution_bitcast_fusion.5
  504.1 9.1 fusion.122
  518.3 8.2 convolution_bitcast_fusion.5
  540.5 9.1 fusion.122
  554.7 8.2 convolution_bitcast_fusion.5
  576.8 9.1 fusion.122
  591.0 8.2 convolution_bitcast_fusion.5
  613.1 9.1 fusion.122
  627.4 8.2 convolution_bitcast_fusion.5
  649.5 9.2 fusion.122
  663.7 8.2 convolution_bitcast_fusion.5
  685.9 9.2 fusion.122
  700.2 8.2 convolution_bitcast_fusion.5
  722.3 9.1 fusion.122
  736.5 8.2 convolution_bitcast_fusion.5
  758.6 9.1 fusion.122
  772.8 8.2 convolution_bitcast_fusion.5
  794.9 9.1 fusion.122
  809.1 8.2 convolution_bitcast_fusion.5
  831.3 9.2 fusion.122
  845.5 8.2 convolution_bitcast_fusion.5
  867.7 9.1 fusion.122
  881.9 8.2 convolution_bitcast_fusion.5
  904.0 9.1 fusion.122
  918.2 8.2 convolution_bitcast_fusion.5
  940.3 9.1 fusion.122
  949.4 20.6 %fusion.60 = (bf16[16,64,64,64]{3,1,2,0:T(8,128)(2,1)}, bf16[16,64,64,64]{3,1,2,0:T(8,128)(2,1)S(1)}) fusion(bf16[16,64,64,128]{3,1,2,0:T(8,128)(2,1)} %get-tuple-element.120), kind=kLoop, calls=%fused_computation.117 | loop fusion | bytes 33554432 | tf_op jit(solution)/shard_map/slice | solution.py:156
  970.0 11.6 %copy.89 = bf16[16,64,64,64]{3,2,1,0:T(8,128)(2,1)} copy(bf16[16,64,64,64]{3,1,2,0:T(8,128)(2,1)S(1)} %get-tuple-element.303) | data formatting | bytes 16777216 | tf_op jit(solution)/shard_map/slice | solution.py:153
  981.6 22.6 %reshape.269 = bf16[16,64,4096]{2,1,0:T(8,128)(2,1)} reshape(bf16[16,64,64,64]{3,2,1,0:T(8,128)(2,1)} %copy.89) | data formatting | bytes 16777216 | tf_op jit(solution)/shard_map/reshape | solution.py:153
  1004.2 18.5 %copy.90 = bf16[16,64,64,64]{3,2,1,0:T(8,128)(2,1)} copy(bf16[16,64,64,64]{3,1,2,0:T(8,128)(2,1)} %get-tuple-element.302) | data formatting | bytes 16777216 | tf_op jit(solution)/shard_map/slice | solution.py:156
  1022.7 22.6 %reshape.270 = bf16[16,64,4096]{2,1,0:T(8,128)(2,1)} reshape(bf16[16,64,64,64]{3,2,1,0:T(8,128)(2,1)} %copy.90) | data formatting | bytes 16777216 | tf_op jit(solution)/shard_map/reshape | solution.py:156
  (420 shorter events, 299.1 us)
Async XLA Ops:
  7.2 78.7 %copy-start = (f32[16]{0:T(128)S(1)}, f32[16]{0:T(128)}, u32[]{:S(2)}) copy-start(f32[16]{0:T(128)} %param.12) | copy-start | bytes 196
  69.6 8.0 copy-start.5
  69.6 271.2 %all-to-all-start = ((bf16[16,64,64,128]{3,2,1,0:T(8,128)(2,1)}), bf16[16,64,64,128]{3,2,1,0:T(8,128)(2,1)}, u32[]{:S(2)}, u32[]{:S(2)}) async-start(bf16[16,64,64,128]{3,2,1,0:T(8,128)(2,1)} %select_select_fusion), calls=%async_computation | async-start | bytes 33554432 | tf_op jit(solution)/shard_map/all_to_all | solution.py:139
  77.5 259.4 %all-gather.2.cloned.1.call-start = ((), (), s32[]{:S(2)}) async-start(), calls=%async_computation.1 | async-start | bytes 2506752 | tf_op jit(solution)/shard_map/all_gather | solution.py:142
  77.6 5.6 collective-permute-start
  79.5 5.1 collective-permute-start.1
  83.2 2.7 copy-start.4
  83.2 2.2 copy-start.6
  85.9 73.0 %copy-start.2 = (f32[17]{0:T(128)S(1)}, f32[17]{0:T(128)}, u32[]{:S(2)}) copy-start(f32[17]{0:T(128)} %param.13) | copy-start | bytes 208
  85.9 73.7 %copy-start.7 = (s32[12]{0:T(128)S(1)}, s32[12]{0:T(128)}, u32[]{:S(2)}) copy-start(s32[12]{0:T(128)} %copy-done.6) | copy-start | bytes 148
  389.6 2.7 copy-start.3
  425.9 2.7 copy-start.3
  462.2 2.7 copy-start.3
  498.6 2.7 copy-start.3
  534.9 2.7 copy-start.3
  571.3 2.7 copy-start.3
  607.6 2.7 copy-start.3
  644.0 2.7 copy-start.3
  680.3 2.7 copy-start.3
  716.8 2.7 copy-start.3
  753.1 2.7 copy-start.3
  789.4 2.7 copy-start.3
  825.7 2.7 copy-start.3
  862.1 2.7 copy-start.3
  898.5 2.7 copy-start.3
  934.8 2.7 copy-start.3
  1022.7 22.6 %copy-start.1 = (f32[16]{0:T(128)S(1)}, f32[16]{0:T(128)}, u32[]{:S(2)}) copy-start(f32[16]{0:T(128)} %param.12) | copy-start | bytes 196
Sparse Core Ops, SparseCore 0:
  85.5 251.4 all-gather.1
where the time goes:
time: 1060 us; the launch traced here: 1050 us
  matrix products  511 us (48%)
  local copies, waits for them, and re-layouts  267 us (25%)
  waiting for transfers between devices  177 us (17%)
  other arithmetic  47.7 us (4%)
  loops' own time  22.1 us (2%)
  between operations  14.3 us (1%)
  starting transfers between devices  13.6 us (1%)
    dot_general x48, matrix products, along_depth(): jnp.einsum('ai,ijk->ajk', matrix, field, preferred_element_type=jnp.float32)  219 us
    all_gather x1, waiting for transfers between devices, local(): coarse_plane = lax.all_gather(layered, 'grp', axis=3, tiled=True)  175 us
    dot_general x16, matrix products, fine_velocity(): return jnp.einsum('nibc,ai->nabc', second_pass, matrix, precision=highest)  131 us
    dot_general x48, matrix products, along_rows(): jnp.einsum('bj,ijk->ibk', matrix, field, preferred_element_type=jnp.float32)  77.2 us
    gather x2, local copies, waits for them, and re-layouts, shape_matrix(): picked = up_taps[jnp.clip(tap_index, 0, 15)]  73 us
    dot_general x32, matrix products, along_cells(): jnp.einsum('ijk,kc->ijc', field, paired, preferred_element_type=jnp.float32)  42.3 us
    dynamic_slice x80, local copies, waits for them, and re-layouts, local(): lax.map(per_slot, (mine_rows, weights, owner_ids, columns, slot_live))  41.6 us
    slice x2, local copies, waits for them, and re-layouts, local(): results[:, :, :, brick_edge:]  39.1 us
  transfers between devices with their start and end apart: 4, of which 2 were waited for; matrix products, arithmetic and copies ran while one was open for 8% of the time, Pallas kernels for 0%

commit v1 on v0

v1 whole, which is shorter than its diff:
```python
import functools

import jax
import jax.numpy as jnp
import numpy as np
from jax import lax
from jax.experimental import pallas as pl
from jax.experimental.pallas import tpu as pltpu
from jax.sharding import PartitionSpec as P

step_time = 0.5
highest = lax.Precision.HIGHEST
edge = 64
rows_z = 4
rows_x = 4
f32 = jnp.float32
bf16 = jnp.bfloat16

PITCH = 72
UNROLL = 4
MESH = pl.DeviceIdType.MESH

NEAR = ((0, 1), (0, 3), (1, 0), (3, 0))
DIAGONAL = ((1, 1), (1, 3), (3, 1), (3, 3))
KNIGHT = ((2, 1), (2, 3), (1, 2), (3, 2))
FAR = ((0, 2), (2, 0), (2, 2))
ORDER = ((0, 0),) + NEAR + DIAGONAL + KNIGHT + FAR
COUNT = len(ORDER)


def shape_matrix(up_taps, smooth_taps, window_len):
    row_ids = jnp.arange(edge, dtype=jnp.int32)[:, None, None]
    col_ids = jnp.arange(window_len, dtype=jnp.int32)[None, :, None]
    tap_ids = jnp.arange(17, dtype=jnp.int32)[None, None, :]
    up_ids = jnp.arange(16, dtype=jnp.int32)[None, None, None, :]
    tap_index = row_ids + tap_ids - 8 * col_ids + 12
    chosen = (tap_index[..., None] == up_ids).astype(f32)
    return jnp.sum(chosen * up_taps * smooth_taps[:, None], axis=(2, 3))


def difference_matrix():
    difference = np.zeros((edge, edge), np.float32)
    for r in range(edge):
        lower, upper = max(r - 1, 0), min(r + 1, edge - 1)
        difference[r, upper] += 1.0 / (upper - lower)
        difference[r, lower] -= 1.0 / (upper - lower)
    return difference


def brick(n, in_ref, a2_ref, a1_ref, a0_ref, t_ref, l_ref, dz_ref, dx_ref, out_ref, s1, s2, s3, s4, s5):
    left = lax.broadcasted_iota(jnp.int32, (1, 128), 1) < edge

    a2 = a2_ref[n]
    none = jnp.zeros_like(a2)
    halves = [jnp.where(left, a2, none), jnp.where(left, none, a2)]
    w2 = jnp.concatenate(
        [jnp.concatenate(p, axis=1) for half in halves for p in ((half, none), (none, half))], axis=0
    )

    def x_pass(h, c):
        pieces = []
        for k in range(4):
            at = pl.ds(pl.multiple_of(h * 512 + k * 128, 128), 128)
            pieces.append(jnp.concatenate([in_ref[0, :, at], in_ref[1, :, at]], axis=1))
        res = jnp.dot(jnp.concatenate(pieces, axis=0), w2, preferred_element_type=f32)
        for k in range(4):
            for p in range(2):
                row = pl.multiple_of((h * 8 + 2 * k + p) * PITCH, 8)
                s1[pl.ds(row, 64), :] = res[k * 64 : (k + 1) * 64, p * 128 : (p + 1) * 128]
        return c

    lax.fori_loop(0, 8, x_pass, 0, unroll=UNROLL)

    def y_pass(h, c):
        cols = [s1[pl.ds(h * 8 + i, 64, stride=PITCH), :].astype(bf16) for i in range(8)]
        res = jnp.dot(a1_ref[n], jnp.concatenate(cols, axis=1), preferred_element_type=f32)
        for i in range(8):
            row = pl.multiple_of((h * 8 + i) * PITCH, 8)
            s2[pl.ds(row, 64), :] = res[:, i * 128 : (i + 1) * 128]
        return c

    lax.fori_loop(0, 8, y_pass, 0, unroll=UNROLL)

    def to_rows(x):
        return jnp.concatenate([x[:, i * 128 : (i + 1) * 128] for i in range(8)], axis=0)

    def to_cols(x):
        return jnp.concatenate([x[i * 64 : (i + 1) * 64] for i in range(8)], axis=1)

    def z_pass(h, c):
        cols = [s2[pl.ds(h * 8 + i, 64, stride=PITCH), :].astype(bf16) for i in range(8)]
        j = to_rows(
            jnp.dot(a0_ref[n], jnp.concatenate(cols, axis=1), preferred_element_type=f32)
        )
        at = pl.ds(pl.multiple_of(h * 16, 16), 80)
        v = jnp.dot(l_ref[...], t_ref[at, :], preferred_element_type=f32)
        vz, vy, vx = v[:, :128], v[:, 128:256], v[:, 256:]
        carry_z = jnp.where(left, j, vz * j).astype(bf16)
        carry_y = jnp.where(left, j, vy * j).astype(bf16)
        carry_x = jnp.where(left, j, vx * j).astype(bf16)
        gz = to_rows(jnp.dot(dz_ref[...], to_cols(carry_z), preferred_element_type=f32))
        pairs = jnp.concatenate(
            [
                jnp.concatenate(
                    [carry_x[(2 * k) * 64 : (2 * k + 1) * 64], carry_x[(2 * k + 1) * 64 : (2 * k + 2) * 64]],
                    axis=1,
                )
                for k in range(4)
            ],
            axis=0,
        )
        gp = jnp.dot(pairs, dx_ref[...], preferred_element_type=f32)
        gx = jnp.concatenate(
            [gp[k * 64 : (k + 1) * 64, p * 128 : (p + 1) * 128] for k in range(4) for p in range(2)],
            axis=0,
        )
        upd = jnp.where(left, vz, 1.0) * gz + jnp.where(left, vx, 1.0) * gx
        row = pl.multiple_of(h * 512, 512)
        s3[pl.ds(row, 512), :] = j - step_time * upd
        s4[pl.ds(row, 512), :] = (0.5 * step_time) * jnp.where(left, vy, 1.0)
        s5[pl.ds(row + 64, 512), :] = carry_y.astype(f32)
        return c

    lax.fori_loop(0, 8, z_pass, 0, unroll=UNROLL)
    s5[0:64, :] = 2.0 * s5[64:128, :] - s5[128:192, :]
    s5[65 * 64 : 66 * 64, :] = 2.0 * s5[64 * 64 : 65 * 64, :] - s5[63 * 64 : 64 * 64, :]

    def finish(h, c):
        for k in range(4):
            o = []
            for p in range(2):
                row = pl.multiple_of(h * 512 + (2 * k + p) * 64, 64)
                diff = s5[pl.ds(row + 128, 64), :] - s5[pl.ds(row, 64), :]
                o.append(s3[pl.ds(row, 64), :] - s4[pl.ds(row, 64), :] * diff)
            at = pl.ds(pl.multiple_of(h * 512 + k * 128, 128), 128)
            img = jnp.where(left, o[0], pltpu.roll(o[1], 64, 1))
            mom = jnp.where(left, pltpu.roll(o[0], 64, 1), o[1])
            out_ref[0, :, at] = img.astype(bf16)
            out_ref[1, :, at] = mom.astype(bf16)
        return c

    lax.fori_loop(0, 8, finish, 0, unroll=UNROLL)


def shoot_kernel(
    picks, cols, owners, src_ref, mom_ref, mid_ref, up_ref, down_ref, x_ref, a2_ref, a1_ref, a0_ref,
    l_ref, dz_ref, dx_ref,
    oimg_ref, omom_ref, arr_ref, inter_ref,
    stage, in_buf, out_buf, plane, halo, t_buf, s1, s2, s3, s4, s5,
    send1, recv1, send2, recv2, vsend, vrecv, in_sem, out_sem,
):
    grp, slab = lax.axis_index("grp"), lax.axis_index("slab")
    my_z, my_x = grp // rows_x, grp % rows_x
    slabs = lax.axis_size("slab")

    def at_offset(dz, dx):
        return {"slab": slab, "grp": lax.rem(my_z + dz, rows_z) * rows_x + lax.rem(my_x + dx, rows_x)}

    def at_slab(step):
        return {"slab": lax.rem(slab + step + slabs, slabs), "grp": grp}

    barrier = pltpu.get_barrier_semaphore()
    peers = [at_offset(d, 0) for d in (1, 2, 3)] + [at_offset(0, d) for d in (1, 2, 3)]
    peers += [at_slab(1), at_slab(-1)]
    for peer in peers:
        pl.semaphore_signal(barrier, inc=1, device_id=peer, device_id_type=MESH)
    pl.semaphore_wait(barrier, len(peers))

    def remote(src, dst, send, recv, device):
        return pltpu.make_async_remote_copy(
            src_ref=src, dst_ref=dst, send_sem=send, recv_sem=recv, device_id=device, device_id_type=MESH
        )

    halos = [
        remote(up_ref, halo.at[0], vsend.at[0], vrecv.at[0], at_slab(1)),
        remote(down_ref, halo.at[1], vsend.at[1], vrecv.at[1], at_slab(-1)),
    ]
    for c in halos:
        c.start()

    first, second = {}, {}
    for n, (dz, dx) in enumerate(ORDER):
        if n == 0:
            continue
        both = dz != 0 and dx != 0
        for f in range(2):
            leg1 = at_offset(dz, 0) if (f == 0) == (dz != 0) or dx == 0 else at_offset(0, dx)
            if not both:
                leg1 = at_offset(dz, dx)
            into = inter_ref.at[n, f] if both else arr_ref.at[n, f]
            first[n, f] = remote(stage.at[n, f], into, send1.at[n, f], recv1.at[n, f], leg1)
            if both:
                leg2 = at_offset(0, dx) if f == 0 else at_offset(dz, 0)
                second[n, f] = remote(
                    inter_ref.at[n, f], arr_ref.at[n, f], send2.at[n, f], recv2.at[n, f], leg2
                )

    def put(n, c):
        stage[n, 0] = src_ref[picks[n]]
        stage[n, 1] = mom_ref[picks[n]]
        return c

    def start(copies, ns):
        for n in ns:
            for f in range(2):
                copies[n, f].start()

    def landed(copies, ns):
        for n in ns:
            for f in range(2):
                copies[n, f].wait_recv()

    near, diagonal, knight = range(1, 5), range(5, 9), range(9, 13)
    lax.fori_loop(1, 9, put, 0)
    start(first, near)
    start(first, diagonal)

    for c in halos:
        c.wait()
    piece = mid_ref[...]
    piece = piece + jnp.where(slab > 0, halo[0], jnp.zeros_like(piece))
    piece = piece + jnp.where(slab < slabs - 1, halo[1], jnp.zeros_like(piece))
    plane[my_x, my_z] = piece
    column = [
        remote(plane.at[my_x, my_z], plane.at[my_x, my_z], vsend.at[1 + d], vrecv.at[1 + d], at_offset(d, 0))
        for d in (1, 2, 3)
    ]
    for c in column:
        c.start()
    lax.fori_loop(9, 16, put, 0)
    for c in column:
        c.wait()
    across = [
        remote(plane.at[my_x], plane.at[my_x], vsend.at[4 + d], vrecv.at[4 + d], at_offset(0, d))
        for d in (1, 2, 3)
    ]
    for c in across:
        c.start()
    lax.fori_loop(0, 1, put, 0)
    for c in across:
        c.wait()

    def window(n):
        owner, last = owners[n], rows_z * rows_x - 1
        before, after = jnp.maximum(owner - 1, 0), jnp.minimum(owner + 1, last)
        pieces = [
            plane[before & 3, before >> 2, 6:8].reshape(32, 256),
            plane[owner & 3, owner >> 2].reshape(128, 256),
            plane[after & 3, after >> 2, 0:2].reshape(32, 256),
        ]
        pieces[0] = jnp.where(owner > 0, pieces[0], jnp.zeros_like(pieces[0]))
        pieces[2] = jnp.where(owner < last, pieces[2], jnp.zeros_like(pieces[2]))
        w = jnp.concatenate(pieces, axis=0)
        along = x_ref[cols[n]]
        none = jnp.zeros_like(along)
        upper = jnp.concatenate([along, none], axis=0)
        paired = jnp.concatenate([upper, jnp.concatenate([none, along], axis=0)], axis=1)
        t_buf[:, :256] = jnp.dot(w[:, :128], paired, preferred_element_type=f32).astype(bf16)
        t_buf[:, 256:] = jnp.dot(w[:, 128:], upper, preferred_element_type=f32).astype(bf16)

    def results(n):
        return [
            pltpu.make_async_copy(out_buf.at[f], ref.at[n], out_sem.at[f])
            for f, ref in enumerate((oimg_ref, omom_ref))
        ]

    def before_near():
        landed(first, near)
        start(first, knight)
        landed(first, diagonal)
        start(second, diagonal)

    def before_diagonal():
        landed(second, diagonal)
        landed(first, knight)
        start(second, knight)

    def before_knight():
        landed(first, [15])
        landed(second, knight)
        start(second, [15])

    hooks = {
        1: before_near,
        3: lambda: start(first, [15]),
        5: before_diagonal,
        7: lambda: start(first, [13, 14]),
        9: before_knight,
        13: lambda: landed(first, [13, 14]),
        15: lambda: landed(second, [15]),
    }

    def work(n, c):
        for at, hook in hooks.items():
            pl.when(n == at)(hook)

        @pl.when(n == 0)
        def _():
            in_buf[...] = stage[0]
            window(n)

        @pl.when(n > 0)
        def _():
            fetch = pltpu.make_async_copy(arr_ref.at[n], in_buf, in_sem)
            fetch.start()
            window(n)
            for done in results(n - 1):
                done.wait()
            fetch.wait()

        brick(n, in_buf, a2_ref, a1_ref, a0_ref, t_buf, l_ref, dz_ref, dx_ref, out_buf, s1, s2, s3, s4, s5)
        for out in results(n):
            out.start()
        return c

    lax.fori_loop(0, COUNT, work, 0)
    for done in results(COUNT - 1):
        done.wait()
    for copies in (first, second):
        for c in copies.values():
            c.wait_send()


def place_kernel(info, img_ref, mom_ref, oimg_ref, omom_ref):
    live = info[COUNT + pl.program_id(0)]

    @pl.when(live != 0)
    def _():
        oimg_ref[...] = img_ref[...]
        omom_ref[...] = mom_ref[...]

    @pl.when(live == 0)
    def _():
        oimg_ref[...] = jnp.zeros_like(oimg_ref)
        omom_ref[...] = jnp.zeros_like(omom_ref)


def place(info, image, moment):
    block = (1,) + image.shape[1:]
    return pl.pallas_call(
        place_kernel,
        grid_spec=pltpu.PrefetchScalarGridSpec(
            num_scalar_prefetch=1,
            grid=(COUNT,),
            in_specs=[pl.BlockSpec(block, lambda j, info: (info[j], 0, 0))] * 2,
            out_specs=[pl.BlockSpec(block, lambda j, info: (j, 0, 0))] * 2,
        ),
        out_shape=[jax.ShapeDtypeStruct(image.shape, image.dtype)] * 2,
        compiler_params=pltpu.CompilerParams(vmem_limit_bytes=60 * 1024 * 1024),
        name="place",
    )(info, image, moment)


def local(source, momentum, velocity, up_taps, smooth_taps, weights, slot_brick):
    me = lax.axis_index("grp")
    my_z, my_x = me // rows_x, me % rows_x
    off_z = jnp.array([o[0] for o in ORDER], jnp.int32)
    off_x = jnp.array([o[1] for o in ORDER], jnp.int32)
    targets = ((my_z + off_z) % rows_z) * rows_x + (my_x + off_x) % rows_x
    owners = ((my_z - off_z) % rows_z) * rows_x + (my_x - off_x) % rows_x
    rows = jnp.take(slot_brick, targets, axis=0)
    picks = jnp.sum(jnp.where((rows >> 3) == me, rows & 7, 0), axis=1)

    slot_ids = jnp.take(slot_brick, me, axis=0)
    slot_range = jnp.arange(COUNT, dtype=jnp.int32)
    match = (slot_ids >> 3)[None, :] == owners[:, None]
    slot_of = jnp.sum(jnp.where(match, slot_range[None, :], 0), axis=1)
    cols = jnp.sum(jnp.where(match, slot_ids[None, :] & 7, 0), axis=1)
    block_of = jnp.sum(jnp.where(match, slot_range[:, None], 0), axis=0)
    info = jnp.concatenate([block_of, (slot_ids >= 0).astype(jnp.int32)])

    coarse = edge // 8
    flat = velocity[0].transpose(2, 1, 0, 3).reshape(coarse, coarse, 3 * edge).astype(bf16)
    flat = jnp.pad(flat, ((0, 0), (0, 0), (0, edge)))
    mid = jnp.pad(flat, ((0, 0), (2, 6), (0, 0)))
    up = jnp.pad(flat[:, coarse - 2 :], ((0, 0), (0, 14), (0, 0)))
    down = jnp.pad(flat[:, :2], ((0, 0), (10, 4), (0, 0)))

    matrix = shape_matrix(up_taps, smooth_taps, coarse + 4)
    column_ids = np.arange(8)[:, None, None]
    x_ids = np.arange(edge)[None, :, None]
    places = x_ids == coarse * column_ids - 2 + np.arange(coarse + 4)[None, None, :]
    doubled = jnp.concatenate([matrix, matrix], axis=0).astype(bf16)
    along_x = jnp.einsum(
        "gkj,cj->gkc", places.astype(bf16), doubled, preferred_element_type=f32
    ).astype(bf16)
    padded = jnp.pad(matrix, ((0, 0), (0, 4)))
    left_v = (matrix[:8, :5][:, None, :, None] * padded[None, :, None, :]).reshape(8 * edge, 80)
    left_v = left_v.astype(bf16)

    mats = jnp.take(weights, slot_of, axis=0)
    a0, a1, a2 = (mats[:, :, d * edge : (d + 1) * edge] for d in range(3))
    a2 = jnp.concatenate([a2, a2], axis=1).transpose(0, 2, 1)
    difference = difference_matrix()
    diff_z = jnp.asarray(difference, bf16)
    diff_x = jnp.asarray(np.kron(np.eye(4, dtype=np.float32), difference.T), bf16)

    block = source.shape[1:]
    result = jax.ShapeDtypeStruct((COUNT,) + block, bf16)
    moved = jax.ShapeDtypeStruct((COUNT, 2) + block, bf16)
    cells = edge * edge
    dma = pltpu.SemaphoreType.DMA
    smem, vmem, hbm = (pl.BlockSpec(memory_space=m) for m in (pltpu.SMEM, pltpu.VMEM, pl.ANY))
    image, moment, _, _ = pl.pallas_call(
        shoot_kernel,
        out_shape=[result, result, moved, moved],
        in_specs=[smem] * 3 + [vmem] * 12,
        out_specs=[hbm] * 4,
        scratch_shapes=[
            pltpu.VMEM((COUNT, 2) + block, bf16),
            pltpu.VMEM((2,) + block, bf16),
            pltpu.VMEM((2,) + block, bf16),
            pltpu.VMEM((rows_x, rows_z) + mid.shape, bf16),
            pltpu.VMEM((2,) + mid.shape, bf16),
            pltpu.VMEM((192, 384), bf16),
            pltpu.VMEM((edge * PITCH, 128), f32),
            pltpu.VMEM((edge * PITCH, 128), f32),
            pltpu.VMEM((cells, 128), f32),
            pltpu.VMEM((cells, 128), f32),
            pltpu.VMEM((cells + 128, 128), f32),
            dma((COUNT, 2)),
            dma((COUNT, 2)),
            dma((COUNT, 2)),
            dma((COUNT, 2)),
            dma((8,)),
            dma((8,)),
            dma,
            dma((2,)),
        ],
        compiler_params=pltpu.CompilerParams(
            collective_id=0, has_side_effects=True, vmem_limit_bytes=58 * 1024 * 1024
        ),
        name="shoot",
    )(picks, cols, owners, source, momentum, mid, up, down, along_x, a2, a1, a0, left_v, diff_z, diff_x)
    return tuple(place(info, image, moment))


def solution(mesh):
    placed = (
        P(("slab", "grp"), None, None),
        P(("slab", "grp"), None, None),
        P(None, None, "slab", "grp", None),
        P(),
        P(),
        P(("slab", "grp"), None, None),
        P("slab", None),
    )
    return jax.shard_map(
        local,
        mesh=mesh,
        in_specs=placed,
        out_specs=(P(("slab", "grp"), None, None), P(("slab", "grp"), None, None)),
        check_vma=False,
    )
```

time: 1060 us -> 291 us (0.27)
  matrix products: 511 us -> 1.65 us
  Pallas kernels: 0 us -> 274 us
  local copies, waits for them, and re-layouts: 267 us -> 6.72 us
  waiting for transfers between devices: 177 us -> 0 us
  other arithmetic: 47.7 us -> 5.88 us
  loops' own time: 22.1 us -> 0 us
  starting transfers between devices: 13.6 us -> 0 us
  between operations: 14.3 us -> 0.81 us
    dot_general x176 -> x1, matrix products: 511 us -> 1.65 us  [local(): jnp.einsum('gkj,cj->gkc', places.astype(bf16), doubled, preferred_element...]
    pallas_call x0 -> x2, Pallas kernels: none -> 274 us  [the longest x1 259 us: local(): pl.pallas_call(shoot_kernel, out_shape=[result, result, moved, moved], in...]
    all_gather x1 -> x0, waiting for transfers between devices: 175 us -> none  [local(): coarse_plane = lax.all_gather(layered, 'grp', axis=3, tiled=True)]
    gather x5 -> x2, local copies, waits for them, and re-layouts: 97.2 us -> 1.84 us  [the longest x1 1.26 us: local(): rows = jnp.take(slot_brick, targets, axis=0)]
    reshape x4 -> x0, local copies, waits for them, and re-layouts: 70.2 us -> none  [the longest x1 22.6 us: local(): results[:, :, :, brick_edge:]]
    slice x4 -> x3, local copies, waits for them, and re-layouts: 50.7 us -> 1.01 us  [the longest x1 0.98 us: local(): a0, a1, a2 = (mats[:, :, d * edge:(d + 1) * edge] for d in range(3))]
    dynamic_slice x80 -> x0, local copies, waits for them, and re-layouts: 41.6 us -> none  [local(): lax.map(per_slot, (mine_rows, weights, owner_ids, columns, slot_live))]
    select_n x6 -> x2, other arithmetic: 29.3 us -> 0.12 us  [local(): mats = jnp.take(weights, slot_of, axis=0)]
  transfers between devices with their start and end apart: 4 -> 0, of which waited for: 2 -> 0; matrix products, arithmetic and copies ran while one was open for 8% -> 0% of each run, Pallas kernels for 0% -> 0%
where the time goes in v1:
time: 291 us; the launch traced here: 289 us
  Pallas kernels  274 us (94%)
  local copies, waits for them, and re-layouts  6.72 us (2%)
  other arithmetic  5.88 us (2%)
    pallas_call x1, Pallas kernels, local(): pl.pallas_call(shoot_kernel, out_shape=[result, result, moved, moved], in...  259 us
    pallas_call x1, Pallas kernels, place(): pl.pallas_call(place_kernel, grid_spec=pltpu.PrefetchScalarGridSpec(num_s...  14.8 us

profile of v1, /device:TPU:16, one launch (start us, length us, event | category | flops | bytes accessed | tf_op | source)
XLA Modules:
  0.0 288.8 jit_solution(16086280128123204880)
XLA Ops:
  0.6 0.0 copy-start
  0.7 0.7 and_bitcast_fusion
  1.4 0.7 fusion.6.owners
  2.1 0.0 copy-start.2
  2.1 0.7 compare_and_fusion.1
  2.8 1.3 gather_fusion
  4.1 0.8 fusion.3
  4.9 0.6 pad_add_fusion.info
  5.5 0.9 convert_bitcast_fusion
  6.5 0.1 convert_element_type.41
  6.6 0.6 pad.21.mid_ref
  7.3 0.6 pad.23.down_ref
  7.9 0.6 pad.22.up_ref
  8.5 0.1 subtract_add_fusion
  8.6 1.0 multiply_reduce_fusion
  9.7 1.6 fusion.x_ref
  11.3 0.1 multiply_convert_fusion
  11.4 0.2 convert_element_type.45
  11.6 0.7 copy.23.l_ref
  12.3 0.0 copy-done
  12.3 0.6 gather_fusion.1
  12.9 0.1 broadcast_select_fusion
  13.0 1.0 fusion.17
  14.0 0.1 maximum_bitcast_fusion
  14.1 0.9 copy.22.a2_ref
  15.0 0.0 copy-done.2
  15.0 258.9 %shoot.1 = (bf16[16,64,4096]{2,1,0:T(8,128)(2,1)}, bf16[16,64,4096]{2,1,0:T(8,128)(2,1)}, bf16[16,2,64,4096]{3,2,1,0:T(8,128)(2,1)}, bf16[16,2,64,4096]{3,2,1,0:T(8,128)(2,1)}) custom-call(s32[16]{0:T(128)} %get-tuple-element.29.picks, s32[16]{0:T(128)} %get-tuple-element.18.cols, s32[16]{0:T(128)} %copy-done.2, bf16[8,64,4096]{2,1,0:T(8,128)(2,1)} %src_ref.1, ...), custom_call_target="tpu_custom_call" | custom-call | tf_op jit(solution)/shard_map/shoot/pallas_call | solution.py:404
  274.0 0.0 copy-start.1
  274.0 14.8 %place.1 = (bf16[16,64,4096]{2,1,0:T(8,128)(2,1)}, bf16[16,64,4096]{2,1,0:T(8,128)(2,1)}) custom-call(s32[32]{0:T(128)} %pad_add_fusion.info, bf16[16,64,4096]{2,1,0:T(8,128)(2,1)} %get-tuple-element.4.img_ref, bf16[16,64,4096]{2,1,0:T(8,128)(2,1)} %get-tuple-element.5.mom_ref), custom_call_target="tpu_custom_call" | custom-call | tf_op jit(solution)/shard_map/place/pallas_call | solution.py:340
  288.8 0.0 copy-done.1
  (14 shorter events, 0.1 us)
Async XLA Ops:
  0.6 11.7 %copy-start = (bf16[16,64,192]{2,1,0:T(8,128)(2,1)S(1)}, bf16[16,64,192]{2,1,0:T(8,128)(2,1)}, u32[]{:S(2)}) copy-start(bf16[16,64,192]{2,1,0:T(8,128)(2,1)} %param.17) | copy-start | bytes 1179652
  2.1 12.9 %copy-start.2 = (s32[16]{0:T(128)}, s32[16]{0:T(128)S(1)}, u32[]{:S(2)}) copy-start(s32[16]{0:T(128)S(1)} %fusion.6.owners) | copy-start | bytes 196
  274.0 14.8 %copy-start.1 = (bf16[16,64,192]{2,1,0:T(8,128)(2,1)S(1)}, bf16[16,64,192]{2,1,0:T(8,128)(2,1)}, u32[]{:S(2)}) copy-start(bf16[16,64,192]{2,1,0:T(8,128)(2,1)} %param.17) | copy-start | bytes 1179652

commit v2 on v1

--- a/solution.py
+++ b/solution.py
@@ -17,13 +17,13 @@
 bf16 = jnp.bfloat16
 
 PITCH = 72
-UNROLL = 4
+UNROLL = 8
 MESH = pl.DeviceIdType.MESH
 
 NEAR = ((0, 1), (0, 3), (1, 0), (3, 0))
 DIAGONAL = ((1, 1), (1, 3), (3, 1), (3, 3))
 KNIGHT = ((2, 1), (2, 3), (1, 2), (3, 2))
-FAR = ((0, 2), (2, 0), (2, 2))
+FAR = ((2, 2), (0, 2), (2, 0))
 ORDER = ((0, 0),) + NEAR + DIAGONAL + KNIGHT + FAR
 COUNT = len(ORDER)
 
@@ -143,7 +143,7 @@
 
 
 def shoot_kernel(
-    picks, cols, owners, src_ref, mom_ref, mid_ref, up_ref, down_ref, x_ref, a2_ref, a1_ref, a0_ref,
+    picks, cols, owners, src_ref, mom_ref, mid_ref, edge_ref, x_ref, a2_ref, a1_ref, a0_ref,
     l_ref, dz_ref, dx_ref,
     oimg_ref, omom_ref, arr_ref, inter_ref,
     stage, in_buf, out_buf, plane, halo, t_buf, s1, s2, s3, s4, s5,
@@ -172,8 +172,8 @@
         )
 
     halos = [
-        remote(up_ref, halo.at[0], vsend.at[0], vrecv.at[0], at_slab(1)),
-        remote(down_ref, halo.at[1], vsend.at[1], vrecv.at[1], at_slab(-1)),
+        remote(edge_ref, halo.at[0], vsend.at[0], vrecv.at[0], at_slab(1)),
+        remote(edge_ref, halo.at[1], vsend.at[1], vrecv.at[1], at_slab(-1)),
     ]
     for c in halos:
         c.start()
@@ -211,33 +211,33 @@
                 copies[n, f].wait_recv()
 
     near, diagonal, knight = range(1, 5), range(5, 9), range(9, 13)
-    lax.fori_loop(1, 9, put, 0)
-    start(first, near)
-    start(first, diagonal)
+    for group in (near, diagonal, knight):
+        lax.fori_loop(group[0], group[-1] + 1, put, 0)
+        start(first, group)
 
     for c in halos:
         c.wait()
     piece = mid_ref[...]
-    piece = piece + jnp.where(slab > 0, halo[0], jnp.zeros_like(piece))
-    piece = piece + jnp.where(slab < slabs - 1, halo[1], jnp.zeros_like(piece))
-    plane[my_x, my_z] = piece
-    column = [
-        remote(plane.at[my_x, my_z], plane.at[my_x, my_z], vsend.at[1 + d], vrecv.at[1 + d], at_offset(d, 0))
-        for d in (1, 2, 3)
-    ]
-    for c in column:
+    layer = lax.broadcasted_iota(jnp.int32, piece.shape, 1)
+    below = (layer < 2) & (slab > 0)
+    above = (layer >= 10) & (layer < 12) & (slab < slabs - 1)
+    plane[my_x, my_z] = jnp.where(below, halo[0], jnp.where(above, halo[1], piece))
+    lower, upper = pl.ds(0, 4), pl.ds(4, 4)
+    mine_lower, mine_upper = plane.at[my_x, my_z, lower], plane.at[my_x, my_z, upper]
+    leg1 = [remote(mine_lower, mine_lower, vsend.at[1 + d], vrecv.at[1 + d], at_offset(d, 0)) for d in (1, 2, 3)]
+    leg1 += [remote(mine_upper, mine_upper, vsend.at[4 + d], vrecv.at[4 + d], at_offset(0, d)) for d in (1, 2, 3)]
+    for c in leg1:
         c.start()
-    lax.fori_loop(9, 16, put, 0)
-    for c in column:
+    lax.fori_loop(13, 16, put, 0)
+    for c in leg1:
         c.wait()
-    across = [
-        remote(plane.at[my_x], plane.at[my_x], vsend.at[4 + d], vrecv.at[4 + d], at_offset(0, d))
-        for d in (1, 2, 3)
-    ]
-    for c in across:
+    row_lower, row_upper = plane.at[my_x, :, lower], plane.at[:, my_z, upper]
+    leg2 = [remote(row_lower, row_lower, vsend.at[7 + d], vrecv.at[7 + d], at_offset(0, d)) for d in (1, 2, 3)]
+    leg2 += [remote(row_upper, row_upper, vsend.at[10 + d], vrecv.at[10 + d], at_offset(d, 0)) for d in (1, 2, 3)]
+    for c in leg2:
         c.start()
     lax.fori_loop(0, 1, put, 0)
-    for c in across:
+    for c in leg2:
         c.wait()
 
     def window(n):
@@ -265,50 +265,63 @@
         ]
 
     def before_near():
-        landed(first, near)
-        start(first, knight)
         landed(first, diagonal)
         start(second, diagonal)
+        start(first, [13])
+        landed(first, near)
 
     def before_diagonal():
-        landed(second, diagonal)
         landed(first, knight)
         start(second, knight)
+        landed(first, [13])
+        start(second, [13])
+        landed(second, diagonal)
 
     def before_knight():
-        landed(first, [15])
         landed(second, knight)
-        start(second, [15])
+        start(first, [14, 15])
 
     hooks = {
         1: before_near,
-        3: lambda: start(first, [15]),
         5: before_diagonal,
-        7: lambda: start(first, [13, 14]),
         9: before_knight,
-        13: lambda: landed(first, [13, 14]),
-        15: lambda: landed(second, [15]),
+        13: lambda: landed(second, [13]),
+        14: lambda: landed(first, [14, 15]),
     }
+
+    def fetch(n):
+        return pltpu.make_async_copy(arr_ref.at[n], in_buf.at[n % 2], in_sem.at[n % 2])
 
     def work(n, c):
         for at, hook in hooks.items():
             pl.when(n == at)(hook)
 
+        opens = (n == 1) | (n == 5) | (n == 9) | (n == 13) | (n == 14)
+        ends = (n == 0) | (n == 4) | (n == 8) | (n == 12) | (n == 13) | (n == 15)
+
         @pl.when(n == 0)
         def _():
-            in_buf[...] = stage[0]
-            window(n)
+            in_buf[0] = stage[0]
+
+        @pl.when(opens)
+        def _():
+            fetch(n).start()
+
+        window(n)
 
         @pl.when(n > 0)
         def _():
-            fetch = pltpu.make_async_copy(arr_ref.at[n], in_buf, in_sem)
-            fetch.start()
-            window(n)
             for done in results(n - 1):
                 done.wait()
-            fetch.wait()
-
-        brick(n, in_buf, a2_ref, a1_ref, a0_ref, t_buf, l_ref, dz_ref, dx_ref, out_buf, s1, s2, s3, s4, s5)
+            fetch(n).wait()
+
+        @pl.when(jnp.logical_not(ends))
+        def _():
+            fetch(n + 1).start()
+
+        brick(
+            n, in_buf.at[n % 2], a2_ref, a1_ref, a0_ref, t_buf, l_ref, dz_ref, dx_ref, out_buf, s1, s2, s3, s4, s5
+        )
         for out in results(n):
             out.start()
         return c
@@ -321,29 +334,66 @@
             c.wait_send()
 
 
-def place_kernel(info, img_ref, mom_ref, oimg_ref, omom_ref):
-    live = info[COUNT + pl.program_id(0)]
-
-    @pl.when(live != 0)
-    def _():
-        oimg_ref[...] = img_ref[...]
-        omom_ref[...] = mom_ref[...]
-
-    @pl.when(live == 0)
-    def _():
-        oimg_ref[...] = jnp.zeros_like(oimg_ref)
-        omom_ref[...] = jnp.zeros_like(omom_ref)
+def place_kernel(info, img_ref, mom_ref, oimg_ref, omom_ref, held, zeros, in_sem, out_sem):
+    fields = ((img_ref, oimg_ref), (mom_ref, omom_ref))
+
+    def read(j, f):
+        return pltpu.make_async_copy(fields[f][0].at[info[j]], held.at[j, f], in_sem.at[j, f])
+
+    def write(j, f, source):
+        return pltpu.make_async_copy(source, fields[f][1].at[j], out_sem.at[j, f])
+
+    def begin(j, c):
+        @pl.when(info[COUNT + j] != 0)
+        def _():
+            read(j, 0).start()
+            read(j, 1).start()
+
+        return c
+
+    lax.fori_loop(0, COUNT, begin, 0)
+    zeros[...] = jnp.zeros_like(zeros)
+
+    def move(j, c):
+        @pl.when(info[COUNT + j] != 0)
+        def _():
+            for f in range(2):
+                read(j, f).wait()
+                write(j, f, held.at[j, f]).start()
+
+        @pl.when(info[COUNT + j] == 0)
+        def _():
+            for f in range(2):
+                write(j, f, zeros).start()
+
+        return c
+
+    lax.fori_loop(0, COUNT, move, 0)
+
+    def end(j, c):
+        for f in range(2):
+            write(j, f, zeros).wait()
+        return c
+
+    lax.fori_loop(0, COUNT, end, 0)
 
 
 def place(info, image, moment):
-    block = (1,) + image.shape[1:]
+    block = image.shape[1:]
+    hbm = pl.BlockSpec(memory_space=pl.ANY)
     return pl.pallas_call(
         place_kernel,
         grid_spec=pltpu.PrefetchScalarGridSpec(
             num_scalar_prefetch=1,
-            grid=(COUNT,),
-            in_specs=[pl.BlockSpec(block, lambda j, info: (info[j], 0, 0))] * 2,
-            out_specs=[pl.BlockSpec(block, lambda j, info: (j, 0, 0))] * 2,
+            grid=(1,),
+            in_specs=[hbm] * 2,
+            out_specs=[hbm] * 2,
+            scratch_shapes=[
+                pltpu.VMEM((COUNT, 2) + block, bf16),
+                pltpu.VMEM(block, bf16),
+                pltpu.SemaphoreType.DMA((COUNT, 2)),
+                pltpu.SemaphoreType.DMA((COUNT, 2)),
+            ],
         ),
         out_shape=[jax.ShapeDtypeStruct(image.shape, image.dtype)] * 2,
         compiler_params=pltpu.CompilerParams(vmem_limit_bytes=60 * 1024 * 1024),
@@ -373,8 +423,7 @@
     flat = velocity[0].transpose(2, 1, 0, 3).reshape(coarse, coarse, 3 * edge).astype(bf16)
     flat = jnp.pad(flat, ((0, 0), (0, 0), (0, edge)))
     mid = jnp.pad(flat, ((0, 0), (2, 6), (0, 0)))
-    up = jnp.pad(flat[:, coarse - 2 :], ((0, 0), (0, 14), (0, 0)))
-    down = jnp.pad(flat[:, :2], ((0, 0), (10, 4), (0, 0)))
+    edges = jnp.roll(mid, 8, axis=1)
 
     matrix = shape_matrix(up_taps, smooth_taps, coarse + 4)
     column_ids = np.arange(8)[:, None, None]
@@ -404,11 +453,11 @@
     image, moment, _, _ = pl.pallas_call(
         shoot_kernel,
         out_shape=[result, result, moved, moved],
-        in_specs=[smem] * 3 + [vmem] * 12,
+        in_specs=[smem] * 3 + [vmem] * 11,
         out_specs=[hbm] * 4,
         scratch_shapes=[
             pltpu.VMEM((COUNT, 2) + block, bf16),
-            pltpu.VMEM((2,) + block, bf16),
+            pltpu.VMEM((2, 2) + block, bf16),
             pltpu.VMEM((2,) + block, bf16),
             pltpu.VMEM((rows_x, rows_z) + mid.shape, bf16),
             pltpu.VMEM((2,) + mid.shape, bf16),
@@ -422,16 +471,16 @@
             dma((COUNT, 2)),
             dma((COUNT, 2)),
             dma((COUNT, 2)),
-            dma((8,)),
-            dma((8,)),
-            dma,
+            dma((14,)),
+            dma((14,)),
+            dma((2,)),
             dma((2,)),
         ],
         compiler_params=pltpu.CompilerParams(
             collective_id=0, has_side_effects=True, vmem_limit_bytes=58 * 1024 * 1024
         ),
         name="shoot",
-    )(picks, cols, owners, source, momentum, mid, up, down, along_x, a2, a1, a0, left_v, diff_z, diff_x)
+    )(picks, cols, owners, source, momentum, mid, edges, along_x, a2, a1, a0, left_v, diff_z, diff_x)
     return tuple(place(info, image, moment))
 
 

time: 291 us -> 268 us (0.921)
  the two profiles are of different devices: /device:TPU:16 before, /device:TPU:64 now
where the time goes in v2:
time: 268 us
  Pallas kernels  253 us (94%)
  other arithmetic  6.49 us (2%)
  local copies, waits for them, and re-layouts  5.47 us (2%)
    pallas_call x1, Pallas kernels, local(): pl.pallas_call(shoot_kernel, out_shape=[result, result, moved, moved], in...  240 us
    pallas_call x1, Pallas kernels, place(): pl.pallas_call(place_kernel, grid_spec=pltpu.PrefetchScalarGridSpec(num_s...  13.1 us

profile of v2, /device:TPU:64, one launch (start us, length us, event | category | flops | bytes accessed | tf_op | source)
XLA Modules:
  0.0 267.7 jit_solution(8555357314115273186)
XLA Ops:
  0.6 0.0 copy-start
  0.7 0.7 and_bitcast_fusion
  1.4 0.7 fusion.6.owners
  2.1 0.0 copy-start.2
  2.1 0.7 compare_and_fusion.1
  2.8 1.3 gather_fusion
  4.1 0.7 fusion.3
  4.8 0.7 pad_add_fusion.info
  5.5 0.9 convert_bitcast_fusion
  6.5 0.1 convert_element_type.37
  6.6 0.6 pad.27.mid_ref
  7.2 0.6 pad_maximum_fusion.edge_ref
  7.8 0.1 subtract_add_fusion
  7.9 1.0 multiply_reduce_fusion
  9.0 1.6 fusion.x_ref
  10.6 0.1 multiply_convert_fusion
  10.7 0.2 convert_element_type.41
  10.9 0.7 copy.23.l_ref
  11.7 0.0 copy-done
  11.7 0.6 gather_fusion.1
  12.2 0.1 broadcast_select_fusion
  12.4 1.0 fusion.17
  13.4 0.1 maximum_bitcast_fusion
  13.5 0.9 copy.22.a2_ref
  14.4 0.0 copy-done.2
  14.4 240.1 %shoot.1 = (bf16[16,64,4096]{2,1,0:T(8,128)(2,1)}, bf16[16,64,4096]{2,1,0:T(8,128)(2,1)}, bf16[16,2,64,4096]{3,2,1,0:T(8,128)(2,1)}, bf16[16,2,64,4096]{3,2,1,0:T(8,128)(2,1)}) custom-call(s32[16]{0:T(128)} %get-tuple-element.29.picks, s32[16]{0:T(128)} %get-tuple-element.18.cols, s32[16]{0:T(128)} %copy-done.2, bf16[8,64,4096]{2,1,0:T(8,128)(2,1)} %src_ref.1, ...), custom_call_target="tpu_custom_call" | custom-call | tf_op jit(solution)/shard_map/shoot/pallas_call | solution.py:453
  254.5 0.0 copy-start.1
  254.5 13.1 %place.1 = (bf16[16,64,4096]{2,1,0:T(8,128)(2,1)}, bf16[16,64,4096]{2,1,0:T(8,128)(2,1)}) custom-call(s32[32]{0:T(128)} %pad_add_fusion.info, bf16[16,64,4096]{2,1,0:T(8,128)(2,1)} %get-tuple-element.4.img_ref, bf16[16,64,4096]{2,1,0:T(8,128)(2,1)} %get-tuple-element.5.mom_ref), custom_call_target="tpu_custom_call" | custom-call | tf_op jit(solution)/shard_map/place/pallas_call | solution.py:384
  267.7 0.0 copy-done.1
  (13 shorter events, 0.1 us)
Async XLA Ops:
  0.6 11.0 %copy-start = (bf16[16,64,192]{2,1,0:T(8,128)(2,1)S(1)}, bf16[16,64,192]{2,1,0:T(8,128)(2,1)}, u32[]{:S(2)}) copy-start(bf16[16,64,192]{2,1,0:T(8,128)(2,1)} %param.17) | copy-start | bytes 1179652
  2.1 12.3 %copy-start.2 = (s32[16]{0:T(128)}, s32[16]{0:T(128)S(1)}, u32[]{:S(2)}) copy-start(s32[16]{0:T(128)S(1)} %fusion.6.owners) | copy-start | bytes 196
  254.5 13.1 %copy-start.1 = (bf16[16,64,192]{2,1,0:T(8,128)(2,1)S(1)}, bf16[16,64,192]{2,1,0:T(8,128)(2,1)}, u32[]{:S(2)}) copy-start(bf16[16,64,192]{2,1,0:T(8,128)(2,1)} %param.17) | copy-start | bytes 1179652

commit v3 on v2

--- a/solution.py
+++ b/solution.py
@@ -22,9 +22,10 @@
 
 NEAR = ((0, 1), (0, 3), (1, 0), (3, 0))
 DIAGONAL = ((1, 1), (1, 3), (3, 1), (3, 3))
-KNIGHT = ((2, 1), (2, 3), (1, 2), (3, 2))
-FAR = ((2, 2), (0, 2), (2, 0))
-ORDER = ((0, 0),) + NEAR + DIAGONAL + KNIGHT + FAR
+CORNER = ((2, 2),)
+KNIGHT = ((2, 1), (1, 2), (2, 3), (3, 2))
+FAR = ((0, 2), (2, 0))
+ORDER = ((0, 0),) + NEAR + DIAGONAL + CORNER + KNIGHT + FAR
 COUNT = len(ORDER)
 
 
@@ -210,7 +211,7 @@
             for f in range(2):
                 copies[n, f].wait_recv()
 
-    near, diagonal, knight = range(1, 5), range(5, 9), range(9, 13)
+    near, diagonal, corner, knight = range(1, 5), range(5, 9), [9], range(10, 14)
     for group in (near, diagonal, knight):
         lax.fori_loop(group[0], group[-1] + 1, put, 0)
         start(first, group)
@@ -228,7 +229,8 @@
     leg1 += [remote(mine_upper, mine_upper, vsend.at[4 + d], vrecv.at[4 + d], at_offset(0, d)) for d in (1, 2, 3)]
     for c in leg1:
         c.start()
-    lax.fori_loop(13, 16, put, 0)
+    lax.fori_loop(9, 10, put, 0)
+    lax.fori_loop(14, 16, put, 0)
     for c in leg1:
         c.wait()
     row_lower, row_upper = plane.at[my_x, :, lower], plane.at[:, my_z, upper]
@@ -267,26 +269,28 @@
     def before_near():
         landed(first, diagonal)
         start(second, diagonal)
-        start(first, [13])
+        start(first, corner)
         landed(first, near)
 
     def before_diagonal():
         landed(first, knight)
         start(second, knight)
-        landed(first, [13])
-        start(second, [13])
+        landed(first, corner)
+        start(second, corner)
         landed(second, diagonal)
 
     def before_knight():
-        landed(second, knight)
+        landed(second, knight[:2])
         start(first, [14, 15])
 
     hooks = {
         1: before_near,
         5: before_diagonal,
-        9: before_knight,
-        13: lambda: landed(second, [13]),
-        14: lambda: landed(first, [14, 15]),
+        9: lambda: landed(second, corner),
+        10: before_knight,
+        12: lambda: landed(second, knight[2:]),
+        14: lambda: landed(first, [14]),
+        15: lambda: landed(first, [15]),
     }
 
     def fetch(n):
@@ -296,8 +300,10 @@
         for at, hook in hooks.items():
             pl.when(n == at)(hook)
 
-        opens = (n == 1) | (n == 5) | (n == 9) | (n == 13) | (n == 14)
-        ends = (n == 0) | (n == 4) | (n == 8) | (n == 12) | (n == 13) | (n == 15)
+        opens, ends = n < 0, n == COUNT - 1
+        for at in (1, 5, 9, 10, 12, 14, 15):
+            opens = opens | (n == at)
+            ends = ends | (n == at - 1)
 
         @pl.when(n == 0)
         def _():

time: 268 us -> 253 us (0.944)
  the two profiles are of different devices: /device:TPU:64 before, /device:TPU:16 now
where the time goes in v3:
time: 253 us; the launch traced here: 249 us
  Pallas kernels  234 us (92%)
  other arithmetic  6.49 us (3%)
  local copies, waits for them, and re-layouts  5.47 us (2%)
    pallas_call x1, Pallas kernels, local(): pl.pallas_call(shoot_kernel, out_shape=[result, result, moved, moved], in...  224 us
    pallas_call x1, Pallas kernels, place(): pl.pallas_call(place_kernel, grid_spec=pltpu.PrefetchScalarGridSpec(num_s...  10.2 us

profile of v3, /device:TPU:16, one launch (start us, length us, event | category | flops | bytes accessed | tf_op | source)
XLA Modules:
  0.0 248.9 jit_solution(1938252869503073994)
XLA Ops:
  0.6 0.0 copy-start
  0.7 0.7 and_bitcast_fusion
  1.4 0.7 fusion.6.owners
  2.1 0.0 copy-start.2
  2.1 0.7 compare_and_fusion.1
  2.8 1.3 gather_fusion
  4.1 0.7 fusion.3
  4.8 0.7 pad_add_fusion.info
  5.5 0.9 convert_bitcast_fusion
  6.5 0.1 convert_element_type.37
  6.6 0.6 pad.27.mid_ref
  7.2 0.6 pad_maximum_fusion.edge_ref
  7.8 0.1 subtract_add_fusion
  7.9 1.0 multiply_reduce_fusion
  9.0 1.6 fusion.x_ref
  10.6 0.1 multiply_convert_fusion
  10.7 0.2 convert_element_type.41
  10.9 0.7 copy.23.l_ref
  11.7 0.0 copy-done
  11.7 0.6 gather_fusion.1
  12.2 0.1 broadcast_select_fusion
  12.4 1.0 fusion.17
  13.4 0.1 maximum_bitcast_fusion
  13.5 0.9 copy.22.a2_ref
  14.4 0.0 copy-done.2
  14.4 224.3 %shoot.1 = (bf16[16,64,4096]{2,1,0:T(8,128)(2,1)}, bf16[16,64,4096]{2,1,0:T(8,128)(2,1)}, bf16[16,2,64,4096]{3,2,1,0:T(8,128)(2,1)}, bf16[16,2,64,4096]{3,2,1,0:T(8,128)(2,1)}) custom-call(s32[16]{0:T(128)} %get-tuple-element.29.picks, s32[16]{0:T(128)} %get-tuple-element.18.cols, s32[16]{0:T(128)} %copy-done.2, bf16[8,64,4096]{2,1,0:T(8,128)(2,1)} %src_ref.1, ...), custom_call_target="tpu_custom_call" | custom-call | tf_op jit(solution)/shard_map/shoot/pallas_call | solution.py:459
  238.7 0.0 copy-start.1
  238.7 10.2 %place.1 = (bf16[16,64,4096]{2,1,0:T(8,128)(2,1)}, bf16[16,64,4096]{2,1,0:T(8,128)(2,1)}) custom-call(s32[32]{0:T(128)} %pad_add_fusion.info, bf16[16,64,4096]{2,1,0:T(8,128)(2,1)} %get-tuple-element.4.img_ref, bf16[16,64,4096]{2,1,0:T(8,128)(2,1)} %get-tuple-element.5.mom_ref), custom_call_target="tpu_custom_call" | custom-call | tf_op jit(solution)/shard_map/place/pallas_call | solution.py:390
  248.9 0.0 copy-done.1
  (13 shorter events, 0.1 us)
Async XLA Ops:
  0.6 11.0 %copy-start = (bf16[16,64,192]{2,1,0:T(8,128)(2,1)S(1)}, bf16[16,64,192]{2,1,0:T(8,128)(2,1)}, u32[]{:S(2)}) copy-start(bf16[16,64,192]{2,1,0:T(8,128)(2,1)} %param.17) | copy-start | bytes 1179652
  2.1 12.3 %copy-start.2 = (s32[16]{0:T(128)}, s32[16]{0:T(128)S(1)}, u32[]{:S(2)}) copy-start(s32[16]{0:T(128)S(1)} %fusion.6.owners) | copy-start | bytes 196
  238.7 10.2 %copy-start.1 = (bf16[16,64,192]{2,1,0:T(8,128)(2,1)S(1)}, bf16[16,64,192]{2,1,0:T(8,128)(2,1)}, u32[]{:S(2)}) copy-start(bf16[16,64,192]{2,1,0:T(8,128)(2,1)} %param.17) | copy-start | bytes 1179652

commit v4 on v3

--- a/solution.py
+++ b/solution.py
@@ -279,15 +279,15 @@
         start(second, corner)
         landed(second, diagonal)
 
-    def before_knight():
-        landed(second, knight[:2])
+    def before_corner():
+        landed(second, corner)
         start(first, [14, 15])
 
     hooks = {
         1: before_near,
         5: before_diagonal,
-        9: lambda: landed(second, corner),
-        10: before_knight,
+        9: before_corner,
+        10: lambda: landed(second, knight[:2]),
         12: lambda: landed(second, knight[2:]),
         14: lambda: landed(first, [14]),
         15: lambda: landed(first, [15]),

time: 253 us -> 267 us (1.055)
  the two profiles are of different devices: /device:TPU:16 before, /device:TPU:0 now
where the time goes in v4:
time: 267 us; the launch traced here: 266 us
  Pallas kernels  252 us (94%)
  other arithmetic  6.49 us (2%)
  local copies, waits for them, and re-layouts  5.47 us (2%)
    pallas_call x1, Pallas kernels, local(): pl.pallas_call(shoot_kernel, out_shape=[result, result, moved, moved], in...  239 us
    pallas_call x1, Pallas kernels, place(): pl.pallas_call(place_kernel, grid_spec=pltpu.PrefetchScalarGridSpec(num_s...  13.1 us

profile of v4, /device:TPU:0, one launch (start us, length us, event | category | flops | bytes accessed | tf_op | source)
XLA Modules:
  0.0 266.4 jit_solution(5088887378073489496)
XLA Ops:
  0.6 0.0 copy-start
  0.7 0.7 and_bitcast_fusion
  1.4 0.7 fusion.6.owners
  2.1 0.0 copy-start.2
  2.1 0.7 compare_and_fusion.1
  2.8 1.3 gather_fusion
  4.1 0.7 fusion.3
  4.8 0.7 pad_add_fusion.info
  5.5 0.9 convert_bitcast_fusion
  6.5 0.1 convert_element_type.37
  6.6 0.6 pad.27.mid_ref
  7.2 0.6 pad_maximum_fusion.edge_ref
  7.8 0.1 subtract_add_fusion
  7.9 1.0 multiply_reduce_fusion
  9.0 1.6 fusion.x_ref
  10.6 0.1 multiply_convert_fusion
  10.7 0.2 convert_element_type.41
  10.9 0.7 copy.23.l_ref
  11.7 0.0 copy-done
  11.7 0.6 gather_fusion.1
  12.2 0.1 broadcast_select_fusion
  12.4 1.0 fusion.17
  13.4 0.1 maximum_bitcast_fusion
  13.5 0.9 copy.22.a2_ref
  14.4 0.0 copy-done.2
  14.4 238.9 %shoot.1 = (bf16[16,64,4096]{2,1,0:T(8,128)(2,1)}, bf16[16,64,4096]{2,1,0:T(8,128)(2,1)}, bf16[16,2,64,4096]{3,2,1,0:T(8,128)(2,1)}, bf16[16,2,64,4096]{3,2,1,0:T(8,128)(2,1)}) custom-call(s32[16]{0:T(128)} %get-tuple-element.29.picks, s32[16]{0:T(128)} %get-tuple-element.18.cols, s32[16]{0:T(128)} %copy-done.2, bf16[8,64,4096]{2,1,0:T(8,128)(2,1)} %src_ref.1, ...), custom_call_target="tpu_custom_call" | custom-call | tf_op jit(solution)/shard_map/shoot/pallas_call | solution.py:459
  253.2 0.0 copy-start.1
  253.3 13.1 %place.1 = (bf16[16,64,4096]{2,1,0:T(8,128)(2,1)}, bf16[16,64,4096]{2,1,0:T(8,128)(2,1)}) custom-call(s32[32]{0:T(128)} %pad_add_fusion.info, bf16[16,64,4096]{2,1,0:T(8,128)(2,1)} %get-tuple-element.4.img_ref, bf16[16,64,4096]{2,1,0:T(8,128)(2,1)} %get-tuple-element.5.mom_ref), custom_call_target="tpu_custom_call" | custom-call | tf_op jit(solution)/shard_map/place/pallas_call | solution.py:390
  266.4 0.0 copy-done.1
  (13 shorter events, 0.1 us)
Async XLA Ops:
  0.6 11.0 %copy-start = (bf16[16,64,192]{2,1,0:T(8,128)(2,1)S(1)}, bf16[16,64,192]{2,1,0:T(8,128)(2,1)}, u32[]{:S(2)}) copy-start(bf16[16,64,192]{2,1,0:T(8,128)(2,1)} %param.17) | copy-start | bytes 1179652
  2.1 12.3 %copy-start.2 = (s32[16]{0:T(128)}, s32[16]{0:T(128)S(1)}, u32[]{:S(2)}) copy-start(s32[16]{0:T(128)S(1)} %fusion.6.owners) | copy-start | bytes 196
  253.2 13.1 %copy-start.1 = (bf16[16,64,192]{2,1,0:T(8,128)(2,1)S(1)}, bf16[16,64,192]{2,1,0:T(8,128)(2,1)}, u32[]{:S(2)}) copy-start(bf16[16,64,192]{2,1,0:T(8,128)(2,1)} %param.17) | copy-start | bytes 1179652
